TPU v7x, 256 devices: a whole 4x4x8 slice. The times are simulated.
256 devices in a mesh: blk: 64 (over y, z, x_hi), aux: 4 (over x_lo, core).
Axes of the slice: x: 4 (x_hi: 2, x_lo: 2; x = x_hi * 2 + x_lo), y: 4, z: 8, core: 2. Of those that a mesh axis runs over, the one named last changes fastest.
Arguments:
- basis_three: bfloat16 [256, 512, 12288], P('aux', 'blk'), may hold values from -0.29882812 to 0.29882812
- block_mask: int32 [4, 512, 3], P('aux', 'blk'), may hold values 0 or 1
- density: bfloat16 [32768, 192], P('blk'), as said below
- density_mask: int32 [512, 3], P('blk'), may hold values from 0 to 1, as said below
Outputs:
- exchange: float32 [32768, 192], P(('blk', 'aux'))
Inputs may be any that keep to these rules, and one draw needn't show every extreme that they name: density is symmetric as a full periodic banded matrix. `density_mask`: column 1 is 1 everywhere; column 2 of block l equals column 0 of block l + 1 modulo 512, so the masked density stays symmetric.
All inputs are finite; a program needn't handle non-finite values. No bound on the sum of `block_mask` on one device may be relied on, other than what follows from the above.
Results may differ from a plain program's by a relative error of at most 0.013.
Values may be sent and summed in bfloat16 or wider, within the bound.
A program may use at most 128 MiB of HBM per device.

v0:
```python
import jax
import jax.numpy as jnp
from jax import lax
from jax.sharding import PartitionSpec as P


def padded(block, sides, width):
    for axis, dim in sides:
        count = lax.axis_size(axis)
        forward = [(i, i + 1) for i in range(count - 1)]
        forward.append((count - 1, 0))
        backward = [(target, source) for source, target in forward]
        low = lax.ppermute(
            lax.slice_in_dim(block, block.shape[dim] - width, None, axis=dim), axis, forward
        )
        high = lax.ppermute(lax.slice_in_dim(block, 0, width, axis=dim), axis, backward)
        block = jnp.concatenate([low, block, high], axis=dim)
    return block


def on_device(basis_three, block_mask, density, density_mask):
    aux_rows, row_blocks, merged_width = basis_three.shape
    band_width = density.shape[1]
    block_size = band_width // 3
    row_count = row_blocks * block_size
    groups = block_mask.shape[0]
    sub_rows = 16
    block_marks = block_mask.astype(jnp.bfloat16)
    three_center = (
        basis_three.reshape(groups, block_size, row_blocks, block_size, 3, block_size)
        * block_marks[:, None, :, None, :, None]
    ).reshape(aux_rows, row_blocks, merged_width)
    density_marks = density_mask.astype(jnp.bfloat16)
    density_masked = (
        density.reshape(row_blocks, block_size, 3, block_size) * density_marks[:, None, :, None]
    ).reshape(row_count, band_width)
    density_near = padded(density_masked, (("blk", 0),), block_size).reshape(
        row_blocks + 2, block_size, band_width
    )
    placed = []
    for offset_index in range(3):
        placed.append(
            jnp.pad(
                density_near[offset_index : offset_index + row_blocks],
                ((0, 0), (0, 0), (offset_index * block_size, (2 - offset_index) * block_size)),
            )
        )
    density_band = jnp.concatenate(placed, axis=1)
    extended = padded(three_center, (("blk", 1),), 1)
    lead_blocks = 1
    offsets = (-1, 0, 1)
    grouped = extended.reshape(
        aux_rows // sub_rows, sub_rows, extended.shape[1] * block_size, band_width
    )

    def add_group(totals, aux_slab):
        start_row = lead_blocks * block_size
        own_rows = aux_slab[:, start_row : start_row + row_count].reshape(
            sub_rows, row_blocks, block_size, band_width
        )
        partial_x = jnp.einsum(
            "qrmk,rks->qrms", own_rows, density_band, preferred_element_type=jnp.float32
        )
        x_rounded = partial_x.astype(jnp.bfloat16)
        updated = []
        for position, target in enumerate(offsets):
            first_row = (lead_blocks + target) * block_size
            near_rows = aux_slab[:, first_row : first_row + row_count].reshape(
                sub_rows, row_blocks, block_size, band_width
            )
            piece = x_rounded[..., (target + 1) * block_size : (target + 4) * block_size]
            updated.append(
                totals[position]
                + jnp.einsum("qrms,qrns->rmn", piece, near_rows, preferred_element_type=jnp.float32)
            )
        return (tuple(updated), None)

    zeros_k = tuple(
        (jnp.zeros((row_blocks, block_size, block_size), jnp.float32) for target in offsets)
    )
    k_blocks, unused = lax.scan(add_group, zeros_k, grouped)
    partial_value = jnp.stack(k_blocks, axis=2).reshape(row_count, band_width)
    return lax.psum_scatter(
        partial_value.astype(jnp.bfloat16), "aux", scatter_dimension=0, tiled=True
    ).astype(jnp.float32)


def solution(mesh):
    placed = (P("aux", "blk", None), P("aux", "blk", None), P("blk", None), P("blk", None))
    return jax.shard_map(
        on_device, mesh=mesh, in_specs=placed, out_specs=P(("blk", "aux"), None), check_vma=False
    )
```

profile of v0, /device:TPU:0, one launch (start us, length us, event | category | flops | bytes accessed | tf_op | source)
XLA Modules:
  0.0 328.2 jit_solution(4628284658614462290)
XLA Ops:
  8.0 23.0 %copy_multiply_fusion = bf16[64,8,12288]{2,0,1:T(8,128)(2,1)S(1)} fusion(bf16[64,8,12288]{2,1,0:T(8,128)(2,1)} %param.6, bf16[8,12288]{1,0:T(8,128)(2,1)S(1)} %mul.32), kind=kLoop, calls=%fused_computation.21 | loop fusion | flops 6291456 | bytes 25362432 | tf_op jit(solution)/shard_map/mul | solution.py:30
  31.0 4.5 %copy-done.3 = bf16[64,8,12288]{2,0,1:T(8,128)(2,1)} copy-done((bf16[64,8,12288]{2,0,1:T(8,128)(2,1)}, bf16[64,8,12288]{2,0,1:T(8,128)(2,1)S(1)}, u32[]{:S(2)}) %copy-start.3) | copy-done | bytes 12582936
  35.8 9.1 %collective-permute-start.1 = (bf16[64,1,12288]{2,0,1:T(8,128)(2,1)S(1)}, bf16[64,1,12288]{2,0,1:T(8,128)(2,1)}, u32[]{:S(2)}, u32[]{:S(2)}) collective-permute-start(bf16[64,1,12288]{2,0,1:T(8,128)(2,1)S(1)} %get-tuple-element.79), channel_id=1, source_target_pairs={{4,0},{8,4},{12,8},{16,12},{20,16},{24,20},{28,24},{32,28},{36,32}... | collective-permute-start | bytes 4718600 | tf_op jit(solution)/shard_map/ppermute | solution.py:16
  46.9 7.7 %collective-permute-start.3 = (bf16[64,192]{0,1:T(8,128)(2,1)}, bf16[64,192]{0,1:T(8,128)(2,1)}, u32[]{:S(2)}, u32[]{:S(2)}) collective-permute-start(bf16[64,192]{0,1:T(8,128)(2,1)} %bitcast.4), channel_id=1, source_target_pairs={{4,0},{8,4},{12,8},{16,12},{20,16},{24,20},{28,24},{32,28},{36,32}... | collective-permute-start | bytes 73736 | tf_op jit(solution)/shard_map/ppermute | solution.py:16
  57.6 50.0 %collective-permute-done.2 = bf16[64,192]{0,1:T(8,128)(2,1)} collective-permute-done((bf16[64,192]{0,1:T(8,128)(2,1)}, bf16[64,192]{0,1:T(8,128)(2,1)}, u32[]{:S(2)}, u32[]{:S(2)}) %collective-permute-start.2) | collective-permute-done | bytes 24608 | tf_op jit(solution)/shard_map/ppermute | solution.py:13
  114.5 7.9 %pad_maximum_fusion = bf16[64,10,12288]{2,0,1:T(8,128)(2,1)S(1)} fusion(bf16[64,1,12288]{2,0,1:T(8,128)(2,1)} %collective-permute-done.1, bf16[64,8,12288]{2,0,1:T(8,128)(2,1)} %copy-done.3, bf16[64,1,12288]{2,0,1:T(8,128)(2,1)} %collective-permute-done), kind=kLoop, calls=%fused_computation.20 | loop fusion | flops 15728640 | bytes 31457280 | tf_op jit(solution)/shard_map/concatenate | solution.py:17
  122.5 47.5 %copy.31 = bf16[64,10,12288]{2,1,0:T(8,128)(2,1)} copy(bf16[64,10,12288]{2,0,1:T(8,128)(2,1)S(1)} %pad_maximum_fusion) | data formatting | bytes 31457280 | tf_op jit(solution)/shard_map/concatenate | solution.py:17
  170.0 37.0 %reshape.36 = bf16[4,16,640,192]{3,2,1,0:T(8,128)(2,1)} reshape(bf16[64,10,12288]{2,1,0:T(8,128)(2,1)} %copy.31) | data formatting | bytes 31457280 | tf_op jit(solution)/shard_map/reshape | solution.py:52
  207.0 87.6 %while.15 = (s32[]{:T(128)}, f32[8,64,64]{2,1,0:T(8,128)S(1)}, f32[8,64,64]{2,1,0:T(8,128)S(1)}, f32[8,64,64]{2,1,0:T(8,128)S(1)}, bf16[4,16,640,192]{3,2,1,0:T(...) while((s32[]{:T(128)}, f32[8,64,64]{2,1,0:T(8,128)S(1)}, ...), condition=%wide.region_1.2_spmd.clone, body=%wide.region_0.1_spmd.clone.sunk | while | flops 1613430784 | bytes 121045216 | solution.py:81
  210.1 3.9 %fusion.73 = (bf16[16,512,192]{2,1,0:T(8,128)(2,1)}, bf16[16,512,192]{2,1,0:T(8,128)(2,1)}, bf16[16,512,192]{2,1,0:T(8,128)(2,1)S(1)}) fusion(bf16[16,640,192]{2,1,0:T(8,128)(2,1)S(1)} %dynamic-slice_bitcast_fusion.2), kind=kLoop, calls=%fused_computation.39.clone.1 | loop fusion | bytes 18874368 | tf_op jit(solution)/shard_map/while/body/eval_jaxpr/slice | solution.py:68
  214.0 5.0 %convert_bitcast_fusion.5 = bf16[16,8,64,320]{3,2,0,1:T(8,128)(2,1)} fusion(bf16[16,8,64,192]{3,2,1,0:T(8,128)(2,1)S(1)} %bitcast.65, bf16[8,192,320]{2,1,0:T(8,128)(2,1)S(1)} %get-tuple-element.150), kind=kOutput, calls=%fused_computation.clone.1 | convolution fusion | flops 1009254400 | bytes 9371648 | tf_op jit(solution)/shard_map/while/body/eval_jaxpr/qrmk,rks->qrms/dot_general | solution.py:61
  219.1 4.8 %fusion.74 = f32[8,64,64]{2,1,0:T(8,128)S(1)} fusion(bf16[16,8,64,192]{3,2,1,0:T(8,128)(2,1)} %bitcast.67, bf16[16,8,64,320]{3,2,0,1:T(8,128)(2,1)} %convert_bitcast_fusion.5, f32[8,64,64]{2,1,0:T(8,128)S(1)} %get-tuple-element.138, pred[]{:T(512)S(6)} %compare.36), kind=kOutput, calls=%fused_computation.19.clone.1 | convolution fusion | flops 201392128 | bytes 8650753 | tf_op jit(solution)/shard_map/while/body/eval_jaxpr/qrms,qrns->rmn/dot_general | solution.py:74
  229.0 2.9 dynamic-slice_bitcast_fusion.2
  232.0 3.9 %fusion.73 = (bf16[16,512,192]{2,1,0:T(8,128)(2,1)}, bf16[16,512,192]{2,1,0:T(8,128)(2,1)}, bf16[16,512,192]{2,1,0:T(8,128)(2,1)S(1)}) fusion(bf16[16,640,192]{2,1,0:T(8,128)(2,1)S(1)} %dynamic-slice_bitcast_fusion.2), kind=kLoop, calls=%fused_computation.39.clone.1 | loop fusion | bytes 18874368 | tf_op jit(solution)/shard_map/while/body/eval_jaxpr/slice | solution.py:68
  235.9 5.0 %convert_bitcast_fusion.5 = bf16[16,8,64,320]{3,2,0,1:T(8,128)(2,1)} fusion(bf16[16,8,64,192]{3,2,1,0:T(8,128)(2,1)S(1)} %bitcast.65, bf16[8,192,320]{2,1,0:T(8,128)(2,1)S(1)} %get-tuple-element.150), kind=kOutput, calls=%fused_computation.clone.1 | convolution fusion | flops 1009254400 | bytes 9371648 | tf_op jit(solution)/shard_map/while/body/eval_jaxpr/qrmk,rks->qrms/dot_general | solution.py:61
  240.9 4.8 %fusion.74 = f32[8,64,64]{2,1,0:T(8,128)S(1)} fusion(bf16[16,8,64,192]{3,2,1,0:T(8,128)(2,1)} %bitcast.67, bf16[16,8,64,320]{3,2,0,1:T(8,128)(2,1)} %convert_bitcast_fusion.5, f32[8,64,64]{2,1,0:T(8,128)S(1)} %get-tuple-element.138, pred[]{:T(512)S(6)} %compare.36), kind=kOutput, calls=%fused_computation.19.clone.1 | convolution fusion | flops 201392128 | bytes 8650753 | tf_op jit(solution)/shard_map/while/body/eval_jaxpr/qrms,qrns->rmn/dot_general | solution.py:74
  250.9 2.9 dynamic-slice_bitcast_fusion.2
  253.8 3.9 %fusion.73 = (bf16[16,512,192]{2,1,0:T(8,128)(2,1)}, bf16[16,512,192]{2,1,0:T(8,128)(2,1)}, bf16[16,512,192]{2,1,0:T(8,128)(2,1)S(1)}) fusion(bf16[16,640,192]{2,1,0:T(8,128)(2,1)S(1)} %dynamic-slice_bitcast_fusion.2), kind=kLoop, calls=%fused_computation.39.clone.1 | loop fusion | bytes 18874368 | tf_op jit(solution)/shard_map/while/body/eval_jaxpr/slice | solution.py:68
  257.7 5.0 %convert_bitcast_fusion.5 = bf16[16,8,64,320]{3,2,0,1:T(8,128)(2,1)} fusion(bf16[16,8,64,192]{3,2,1,0:T(8,128)(2,1)S(1)} %bitcast.65, bf16[8,192,320]{2,1,0:T(8,128)(2,1)S(1)} %get-tuple-element.150), kind=kOutput, calls=%fused_computation.clone.1 | convolution fusion | flops 1009254400 | bytes 9371648 | tf_op jit(solution)/shard_map/while/body/eval_jaxpr/qrmk,rks->qrms/dot_general | solution.py:61
  262.7 4.9 %fusion.74 = f32[8,64,64]{2,1,0:T(8,128)S(1)} fusion(bf16[16,8,64,192]{3,2,1,0:T(8,128)(2,1)} %bitcast.67, bf16[16,8,64,320]{3,2,0,1:T(8,128)(2,1)} %convert_bitcast_fusion.5, f32[8,64,64]{2,1,0:T(8,128)S(1)} %get-tuple-element.138, pred[]{:T(512)S(6)} %compare.36), kind=kOutput, calls=%fused_computation.19.clone.1 | convolution fusion | flops 201392128 | bytes 8650753 | tf_op jit(solution)/shard_map/while/body/eval_jaxpr/qrms,qrns->rmn/dot_general | solution.py:74
  275.7 3.9 %fusion.73 = (bf16[16,512,192]{2,1,0:T(8,128)(2,1)}, bf16[16,512,192]{2,1,0:T(8,128)(2,1)}, bf16[16,512,192]{2,1,0:T(8,128)(2,1)S(1)}) fusion(bf16[16,640,192]{2,1,0:T(8,128)(2,1)S(1)} %dynamic-slice_bitcast_fusion.2), kind=kLoop, calls=%fused_computation.39.clone.1 | loop fusion | bytes 18874368 | tf_op jit(solution)/shard_map/while/body/eval_jaxpr/slice | solution.py:68
  279.6 5.0 %convert_bitcast_fusion.5 = bf16[16,8,64,320]{3,2,0,1:T(8,128)(2,1)} fusion(bf16[16,8,64,192]{3,2,1,0:T(8,128)(2,1)S(1)} %bitcast.65, bf16[8,192,320]{2,1,0:T(8,128)(2,1)S(1)} %get-tuple-element.150), kind=kOutput, calls=%fused_computation.clone.1 | convolution fusion | flops 1009254400 | bytes 9371648 | tf_op jit(solution)/shard_map/while/body/eval_jaxpr/qrmk,rks->qrms/dot_general | solution.py:61
  284.6 4.9 %fusion.74 = f32[8,64,64]{2,1,0:T(8,128)S(1)} fusion(bf16[16,8,64,192]{3,2,1,0:T(8,128)(2,1)} %bitcast.67, bf16[16,8,64,320]{3,2,0,1:T(8,128)(2,1)} %convert_bitcast_fusion.5, f32[8,64,64]{2,1,0:T(8,128)S(1)} %get-tuple-element.138, pred[]{:T(512)S(6)} %compare.36), kind=kOutput, calls=%fused_computation.19.clone.1 | convolution fusion | flops 201392128 | bytes 8650753 | tf_op jit(solution)/shard_map/while/body/eval_jaxpr/qrms,qrns->rmn/dot_general | solution.py:74
  296.1 23.6 %reduce-scatter.4.cloned.1.call-done = bf16[128,192]{1,0:T(8,128)(2,1)} async-done(((bf16[512,192]{1,0:T(8,128)(2,1)}), bf16[128,192]{1,0:T(8,128)(2,1)}) %reduce-scatter.4.cloned.1.call-update) | async-done | bytes 49168
  (88 shorter events, 43.0 us)
Async XLA Ops:
  6.5 313.2 %reduce-scatter.4.cloned.1.call-start = ((), (), s32[]{:S(2)}) async-start(), calls=%async_computation.1 | async-start | bytes 327680
  31.0 4.5 %copy-start.3 = (bf16[64,8,12288]{2,0,1:T(8,128)(2,1)}, bf16[64,8,12288]{2,0,1:T(8,128)(2,1)S(1)}, u32[]{:S(2)}) copy-start(bf16[64,8,12288]{2,0,1:T(8,128)(2,1)S(1)} %copy_multiply_fusion) | copy-start | bytes 37748740
  35.5 9.3 %copy-start.8 = (s32[8,3]{0,1:T(4,128)S(1)}, s32[8,3]{0,1:T(4,128)}, u32[]{:S(2)}) copy-start(s32[8,3]{0,1:T(4,128)} %param.9) | copy-start | bytes 292
  35.8 78.8 %collective-permute-start.1 = (bf16[64,1,12288]{2,0,1:T(8,128)(2,1)S(1)}, bf16[64,1,12288]{2,0,1:T(8,128)(2,1)}, u32[]{:S(2)}, u32[]{:S(2)}) collective-permute-start(bf16[64,1,12288]{2,0,1:T(8,128)(2,1)S(1)} %get-tuple-element.79), channel_id=1, source_target_pairs={{4,0},{8,4},{12,8},{16,12},{20,16},{24,20},{28,24},{32,28},{36,32}... | collective-permute-start | bytes 4718600 | tf_op jit(solution)/shard_map/ppermute | solution.py:16
  44.9 69.7 %collective-permute-start = (bf16[64,1,12288]{2,0,1:T(8,128)(2,1)S(1)}, bf16[64,1,12288]{2,0,1:T(8,128)(2,1)}, u32[]{:S(2)}, u32[]{:S(2)}) collective-permute-start(bf16[64,1,12288]{2,0,1:T(8,128)(2,1)S(1)} %get-tuple-element.78), channel_id=1, source_target_pairs={{0,4},{4,8},{8,12},{12,16},{16,20},{20,24},{24,28},{28,32},{32,36}... | collective-permute-start | bytes 4718600 | tf_op jit(solution)/shard_map/ppermute | solution.py:13
  46.9 60.7 %collective-permute-start.2 = (bf16[64,192]{0,1:T(8,128)(2,1)}, bf16[64,192]{0,1:T(8,128)(2,1)}, u32[]{:S(2)}, u32[]{:S(2)}) collective-permute-start(bf16[64,192]{0,1:T(8,128)(2,1)} %bitcast.1), channel_id=1, source_target_pairs={{0,4},{4,8},{8,12},{12,16},{16,20},{20,24},{24,28},{28,32},{32,36}... | collective-permute-start | bytes 73736 | tf_op jit(solution)/shard_map/ppermute | solution.py:13
  46.9 60.7 %collective-permute-start.3 = (bf16[64,192]{0,1:T(8,128)(2,1)}, bf16[64,192]{0,1:T(8,128)(2,1)}, u32[]{:S(2)}, u32[]{:S(2)}) collective-permute-start(bf16[64,192]{0,1:T(8,128)(2,1)} %bitcast.4), channel_id=1, source_target_pairs={{4,0},{8,4},{12,8},{16,12},{20,16},{24,20},{28,24},{32,28},{36,32}... | collective-permute-start | bytes 73736 | tf_op jit(solution)/shard_map/ppermute | solution.py:16
  170.0 37.0 %copy-start.4 = (bf16[8,192,320]{2,1,0:T(8,128)(2,1)S(1)}, bf16[8,192,320]{2,1,0:T(8,128)(2,1)}, u32[]{:S(2)}) copy-start(bf16[8,192,320]{2,1,0:T(8,128)(2,1)} %fusion.49) | copy-start | bytes 2949124
  170.0 37.0 %copy-start.5 = (f32[8,64,64]{2,1,0:T(8,128)S(1)}, f32[8,64,64]{2,1,0:T(8,128)}, u32[]{:S(2)}) copy-start(f32[8,64,64]{2,1,0:T(8,128)} %custom-call.1) | copy-start | bytes 393220
  170.0 37.0 %copy-start.6 = (f32[8,64,64]{2,1,0:T(8,128)S(1)}, f32[8,64,64]{2,1,0:T(8,128)}, u32[]{:S(2)}) copy-start(f32[8,64,64]{2,1,0:T(8,128)} %custom-call.2) | copy-start | bytes 393220
  170.0 37.0 %copy-start.7 = (f32[8,64,64]{2,1,0:T(8,128)S(1)}, f32[8,64,64]{2,1,0:T(8,128)}, u32[]{:S(2)}) copy-start(f32[8,64,64]{2,1,0:T(8,128)} %custom-call) | copy-start | bytes 393220
  214.0 5.0 %copy-start.1 = (bf16[16,512,192]{2,1,0:T(8,128)(2,1)}, bf16[16,512,192]{2,1,0:T(8,128)(2,1)S(1)}, u32[]{:S(2)}) copy-start(bf16[16,512,192]{2,1,0:T(8,128)(2,1)S(1)} %get-tuple-element.127) | copy-start | bytes 9437188 | tf_op jit(solution)/shard_map/while
  219.0 4.9 %copy-start.2 = (bf16[16,512,192]{2,1,0:T(8,128)(2,1)S(1)}, bf16[16,512,192]{2,1,0:T(8,128)(2,1)}, u32[]{:S(2)}) copy-start(bf16[16,512,192]{2,1,0:T(8,128)(2,1)} %copy-done.1) | copy-start | bytes 9437188 | tf_op jit(solution)/shard_map/while
  219.0 6.5 %copy-start.9 = (bf16[16,8,64,320]{3,2,0,1:T(8,128)(2,1)S(1)}, bf16[16,8,64,320]{3,2,0,1:T(8,128)(2,1)}, u32[]{:S(2)}) copy-start(bf16[16,8,64,320]{3,2,0,1:T(8,128)(2,1)} %convert_bitcast_fusion.5) | copy-start | bytes 15728644 | tf_op jit(solution)/shard_map/while
  225.6 2.2 copy-start
  235.9 5.0 %copy-start.1 = (bf16[16,512,192]{2,1,0:T(8,128)(2,1)}, bf16[16,512,192]{2,1,0:T(8,128)(2,1)S(1)}, u32[]{:S(2)}) copy-start(bf16[16,512,192]{2,1,0:T(8,128)(2,1)S(1)} %get-tuple-element.127) | copy-start | bytes 9437188 | tf_op jit(solution)/shard_map/while
  240.9 4.9 %copy-start.2 = (bf16[16,512,192]{2,1,0:T(8,128)(2,1)S(1)}, bf16[16,512,192]{2,1,0:T(8,128)(2,1)}, u32[]{:S(2)}) copy-start(bf16[16,512,192]{2,1,0:T(8,128)(2,1)} %copy-done.1) | copy-start | bytes 9437188 | tf_op jit(solution)/shard_map/while
  240.9 6.5 %copy-start.9 = (bf16[16,8,64,320]{3,2,0,1:T(8,128)(2,1)S(1)}, bf16[16,8,64,320]{3,2,0,1:T(8,128)(2,1)}, u32[]{:S(2)}) copy-start(bf16[16,8,64,320]{3,2,0,1:T(8,128)(2,1)} %convert_bitcast_fusion.5) | copy-start | bytes 15728644 | tf_op jit(solution)/shard_map/while
  257.7 5.0 %copy-start.1 = (bf16[16,512,192]{2,1,0:T(8,128)(2,1)}, bf16[16,512,192]{2,1,0:T(8,128)(2,1)S(1)}, u32[]{:S(2)}) copy-start(bf16[16,512,192]{2,1,0:T(8,128)(2,1)S(1)} %get-tuple-element.127) | copy-start | bytes 9437188 | tf_op jit(solution)/shard_map/while
  262.7 4.9 %copy-start.2 = (bf16[16,512,192]{2,1,0:T(8,128)(2,1)S(1)}, bf16[16,512,192]{2,1,0:T(8,128)(2,1)}, u32[]{:S(2)}) copy-start(bf16[16,512,192]{2,1,0:T(8,128)(2,1)} %copy-done.1) | copy-start | bytes 9437188 | tf_op jit(solution)/shard_map/while
  262.7 6.5 %copy-start.9 = (bf16[16,8,64,320]{3,2,0,1:T(8,128)(2,1)S(1)}, bf16[16,8,64,320]{3,2,0,1:T(8,128)(2,1)}, u32[]{:S(2)}) copy-start(bf16[16,8,64,320]{3,2,0,1:T(8,128)(2,1)} %convert_bitcast_fusion.5) | copy-start | bytes 15728644 | tf_op jit(solution)/shard_map/while
  279.6 5.0 %copy-start.1 = (bf16[16,512,192]{2,1,0:T(8,128)(2,1)}, bf16[16,512,192]{2,1,0:T(8,128)(2,1)S(1)}, u32[]{:S(2)}) copy-start(bf16[16,512,192]{2,1,0:T(8,128)(2,1)S(1)} %get-tuple-element.127) | copy-start | bytes 9437188 | tf_op jit(solution)/shard_map/while
  284.6 4.9 %copy-start.2 = (bf16[16,512,192]{2,1,0:T(8,128)(2,1)S(1)}, bf16[16,512,192]{2,1,0:T(8,128)(2,1)}, u32[]{:S(2)}) copy-start(bf16[16,512,192]{2,1,0:T(8,128)(2,1)} %copy-done.1) | copy-start | bytes 9437188 | tf_op jit(solution)/shard_map/while
  284.6 6.5 %copy-start.9 = (bf16[16,8,64,320]{3,2,0,1:T(8,128)(2,1)S(1)}, bf16[16,8,64,320]{3,2,0,1:T(8,128)(2,1)}, u32[]{:S(2)}) copy-start(bf16[16,8,64,320]{3,2,0,1:T(8,128)(2,1)} %convert_bitcast_fusion.5) | copy-start | bytes 15728644 | tf_op jit(solution)/shard_map/while
  (3 other events, 6.6 us)
Sparse Core Ops, SparseCore 0:
  296.3 23.4 reduce-scatter.3
where the time goes:
time: 333 us; the launch traced here: 328 us
  local copies, waits for them, and re-layouts  136 us (41%)
  waiting for transfers between devices  73.6 us (22%)
  matrix products  50.3 us (15%)
  other arithmetic  37.8 us (11%)
  starting transfers between devices  16.9 us (5%)
  between operations  13.5 us (4%)
    ppermute x2, waiting for transfers between devices, padded(): lax.ppermute(lax.slice_in_dim(block, block.shape[dim] - width, None, axis...  50 us
    concatenate x1, local copies, waits for them, and re-layouts, padded(): block = jnp.concatenate([low, block, high], axis=dim)  47.5 us
    reshape x1, local copies, waits for them, and re-layouts, on_device(): extended.reshape(aux_rows // sub_rows, sub_rows, extended.shape[1] * bloc...  37 us
    dot_general x12, matrix products, add_group(): jnp.einsum('qrms,qrns->rmn', piece, near_rows, preferred_element_type=jnp...  30.3 us
    unnamed x2, waiting for transfers between devices  23.6 us
    mul x1, other arithmetic, on_device(): basis_three.reshape(groups, block_size, row_blocks, block_size, 3, block_...  23 us
    dot_general x4, matrix products, add_group(): jnp.einsum('qrmk,rks->qrms', own_rows, density_band, preferred_element_ty...  20.1 us
    ppermute x2, starting transfers between devices, padded(): lax.ppermute(lax.slice_in_dim(block, 0, width, axis=dim), axis, backward)  16.9 us
  transfers between devices with their start and end apart: 5, of which 2 were waited for; matrix products, arithmetic and copies ran while one was open for 4% of the time, Pallas kernels for 0%

commit v1 on v0

v1 whole, which is shorter than its diff:
```python
import functools

import jax
import jax.numpy as jnp
from jax import lax
from jax.experimental import pallas as pl
from jax.experimental.pallas import tpu as pltpu
from jax.sharding import PartitionSpec as P

MESH = pl.DeviceIdType.MESH
NT = (((1,), (1,)), ((), ()))
BF = jnp.bfloat16
F32 = jnp.float32

NB = 8
BS = 64
CP = 4
NC = 16
NG = NC // 2


def first_place(b):
    return (b + 3) % 4


def aligned(cols, halves, place, low):
    turned = {}

    def at(half, side):
        col = half // 2
        if half % 2 == side:
            return cols[col]
        if col not in turned:
            turned[col] = pltpu.roll(cols[col], BS, 1)
        return turned[col]

    slots = [None] * 4
    for k, half in enumerate(halves):
        slots[(place + k) % 4] = half
    out = []
    for q in range(2):
        left, right = slots[2 * q], slots[2 * q + 1]
        if left is None:
            out.append(at(right, 1))
        elif right is None:
            out.append(at(left, 0))
        else:
            a, b = at(left, 0), at(right, 1)
            out.append(a if a is b else jnp.where(low, a, b))
    return out


def kernel(
    nblk, naux,
    x_hbm, bm_ref, d_hbm, dm_ref, out_ref,
    x_v, d_v, ta, tb, h7, h0, send_l, send_r, recv_r, recv_l, dens, mask, mask_s, halo_s, halo_r,
    k0, k1, kb, xf, xs, r1, c_s, c_r,
    x_sem, d_sem, hs, hr, bs_l, bs_r, br_l, br_r, s1, rs1, s2, rs2,
):
    blk, aux = lax.axis_index("blk"), lax.axis_index("aux")
    right, left = lax.rem(blk + 1, nblk), lax.rem(blk + nblk - 1, nblk)

    def load(c):
        return pltpu.make_async_copy(x_hbm.at[pl.ds(c * CP, CP)], x_v.at[pl.ds(c * CP, CP)], x_sem.at[c])

    density = pltpu.make_async_copy(d_hbm, d_v, d_sem)
    density.start()
    for c in range(NC):
        load(c).start()

    barrier = pltpu.get_barrier_semaphore()
    for where in (left, blk, right):
        for k in range(naux):
            if where is blk and k == 0:
                continue
            pl.semaphore_signal(barrier, inc=1, device_id=(where, lax.rem(aux + k, naux)), device_id_type=MESH)

    lane = lax.broadcasted_iota(jnp.int32, (32, 128), 1)
    low = lane < BS
    low64 = lax.broadcasted_iota(jnp.int32, (BS, 128), 1) < BS

    def lanes_of(values, place, rows):
        spot = lax.broadcasted_iota(jnp.int32, (rows, 256), 1) // BS
        total = jnp.zeros((rows, 256), F32)
        for j, value in enumerate(values):
            total = jnp.where(spot == (place + j) % 4, value, total)
        return total.astype(BF)

    for b in range(NB):
        mask[b] = lanes_of([bm_ref[0, b, j].astype(F32) for j in range(3)], first_place(b), 32)
    for s, b in enumerate((0, NB - 1)):
        m = [bm_ref[0, b, j].astype(F32) for j in range(3)]
        for q, (u, v) in enumerate(((0, 1), (2, 0), (1, 2))):
            mask_s[s, :, q * 128 : (q + 1) * 128] = jnp.where(low, m[u], m[v]).astype(BF)
    hole = [lanes_of([1.0, 1.0, 1.0], first_place(b), 32) for b in (0, NB - 1)]

    density.wait()
    zero = jnp.zeros((BS, 128), BF)

    def rows_of(l):
        cols = [d_v[l * BS : (l + 1) * BS, 0:128], jnp.concatenate([d_v[l * BS : (l + 1) * BS, 128:192], zero[:, 0:BS]], axis=1)]
        m = [dm_ref[l, j].astype(F32) for j in range(3)]
        return [
            cols[0] * jnp.where(low64, m[0], m[1]).astype(BF),
            cols[1] * jnp.where(low64, m[2], 0.0).astype(BF),
        ]

    first, last = rows_of(0), rows_of(NB - 1)
    halo_s[0] = jnp.where(low64, pltpu.roll(first[0], BS, 1), pltpu.roll(first[1], BS, 1))
    halo_s[1] = last[0]

    def to_left(src, dst, ss, rs):
        return pltpu.make_async_remote_copy(src_ref=src, dst_ref=dst, send_sem=ss, recv_sem=rs, device_id=(left, aux), device_id_type=MESH)

    def to_right(src, dst, ss, rs):
        return pltpu.make_async_remote_copy(src_ref=src, dst_ref=dst, send_sem=ss, recv_sem=rs, device_id=(right, aux), device_id_type=MESH)

    halo = (
        to_left(halo_s.at[0], halo_r.at[0], hs.at[0], hr.at[0]),
        to_right(halo_s.at[1], halo_r.at[1], hs.at[1], hr.at[1]),
    )

    def tile_left(g):
        return to_left(send_l.at[g], recv_r.at[g], bs_l.at[g], br_r.at[g])

    def tile_right(g):
        return to_right(send_r.at[g], recv_l.at[g], bs_r.at[g], br_l.at[g])

    def spread(c, t, send, which, g):
        for k in range(CP):
            rows = x_v[c * CP + k].reshape(NB, 32, 384)
            for b in range(NB):
                u = rows[b]
                if b == (0, NB - 1)[which]:
                    send[g, k] = u * mask_s[which]
                cols = [u[:, q * 128 : (q + 1) * 128] for q in range(3)]
                for par in range(2):
                    made = aligned(cols, [3 * par + n for n in range(3)], first_place(b), low)
                    for q in range(2):
                        t[b, k, par * 32 : (par + 1) * 32, q * 128 : (q + 1) * 128] = made[q] * mask[b, :, q * 128 : (q + 1) * 128]

    def pick(o, base):
        s0 = jnp.where(low64, o[base : base + 64, 0:128], o[base + 64 : base + 128, 0:128])
        s1_ = jnp.where(low64, o[base + 128 : base + 192, 128:256], o[base + 192 : base + 256, 128:256])
        return s0 + s1_

    def multiply(t, which, g):
        before = None
        for b in range(NB):
            tile = t[b].reshape(CP * BS, 256)
            half = jnp.dot(tile, dens[b], preferred_element_type=F32).astype(BF)
            if b == 0:
                k0[b] += pick(lax.dot_general(half, tile, NT, preferred_element_type=F32), 0)
                if which == 1:
                    h0[g] = jnp.dot(tile, dens[NB], preferred_element_type=F32).astype(BF)
            else:
                o = lax.dot_general(jnp.concatenate([half, before], axis=0), tile, NT, preferred_element_type=F32)
                k0[b] += pick(o, 0)
                k1[b - 1] += pick(o, 256)
            if b == NB - 1 and which == 0:
                h7[g] = half
            before = half

    load(0).wait()
    spread(0, ta, send_l, 0, 0)
    pl.semaphore_wait(barrier, 3 * naux - 1)
    tile_left(0).start()
    for h in halo:
        h.start()

    k0[...] = jnp.zeros_like(k0)
    k1[...] = jnp.zeros_like(k1)
    kb[...] = jnp.zeros_like(kb)

    def place_rows(b, l, cols, drop):
        at = l % 4
        made = aligned(cols, [0, 1, 2], first_place(l), low64)
        keep = lanes_of([0.0 if drop == j else 1.0 for j in range(3)], first_place(l), BS)
        for q in range(2):
            dens[b, at * BS : (at + 1) * BS, q * 128 : (q + 1) * 128] = made[q] * keep[:, q * 128 : (q + 1) * 128]

    blocks = {l: rows_of(l) for l in range(NB)}
    for b in range(NB):
        at = (b + 2) % 4
        dens[b, at * BS : (at + 1) * BS, :] = jnp.zeros((BS, 256), BF)
        for l in (b - 1, b, b + 1):
            if 0 <= l < NB:
                place_rows(b, l, blocks[l], 0 if l == b - 1 else None)
    dens[NB, 2 * BS : 3 * BS, :] = jnp.zeros((BS, 256), BF)
    place_rows(NB, 0, blocks[0], None)
    place_rows(NB, 1, blocks[1], 2)

    def turned(v):
        full = jnp.concatenate([v.astype(F32), jnp.zeros((BS, 128), F32)], axis=0)
        return full.T[0:BS].astype(BF)

    halo[0].wait_recv()
    halo[1].wait_recv()
    own = turned(last[1])
    middle = pltpu.roll(halo_r[0], BS, 1)
    after = [jnp.where(low64, own, middle), middle]
    place_rows(NB - 1, NB, after, None)
    own = turned(first[0])
    ahead = [halo_r[1], own]
    place_rows(0, -1, ahead, 0)
    place_rows(NB, -1, ahead, None)

    def step(g, carry):
        load(2 * g + 1).wait()
        spread(2 * g + 1, tb, send_r, 1, g)
        multiply(ta, 0, g)
        tile_right(g).start()

        @pl.when(g < NG - 1)
        def _():
            load(2 * g + 2).wait()

        nxt = jnp.minimum(g + 1, NG - 1)
        spread(2 * nxt, ta, send_l if False else send_l, 0, g + 1)
        multiply(tb, 1, g)

        @pl.when(g < NG - 1)
        def _():
            tile_left(g + 1).start()

        return carry

    lax.fori_loop(0, NG, step, 0)

    def folded(a, c):
        return jnp.where(low64, a + pltpu.roll(a, BS, 1), c + pltpu.roll(c, BS, 1))

    r = lax.broadcasted_iota(jnp.int32, (BS, 128), 0)
    c = lax.broadcasted_iota(jnp.int32, (BS, 128), 1)
    row_perm = jnp.where(r == 32 * (c % 2) + c // 2, 1.0, 0.0)[:, 0:BS]
    back = row_perm.T.astype(BF)
    r = lax.broadcasted_iota(jnp.int32, (128, 128), 0)
    c = lax.broadcasted_iota(jnp.int32, (128, 128), 1)
    lane_perm = jnp.where((r % BS == 32 * (c % 2) + (c % BS) // 2) & (r // BS == c // BS), 1.0, 0.0).astype(BF)

    def natural(v):
        v = jnp.dot(v.astype(BF), lane_perm, preferred_element_type=F32).astype(BF)
        return jnp.dot(back, v, preferred_element_type=F32)

    xs[0] = jnp.zeros((BS, 128), BF)
    xf[0] = jnp.zeros((BS, 128), F32)
    for b in range(NB):
        v = natural(folded(k0[b], k1[b]))
        xf[b + 1] = v
        xs[b + 1] = v.astype(BF)
    shares = []
    for k in range(1, naux):
        to = lax.rem(aux + k, naux)
        cp = pltpu.make_async_remote_copy(
            src_ref=xs.at[pl.ds(2 * to, 3)], dst_ref=r1.at[k - 1], send_sem=s1.at[k - 1], recv_sem=rs1.at[k - 1],
            device_id=(blk, to), device_id_type=MESH,
        )
        cp.start()
        shares.append(cp)

    def edge(recv, g, which):
        parts = []
        for k in range(CP):
            u = recv[g, k]
            cols = [u[:, q * 128 : (q + 1) * 128] for q in range(3)]
            for par in range(2):
                made = aligned(cols, [3 * par + n for n in range(3)], first_place((0, NB - 1)[which]), low)
                parts.append(jnp.concatenate([made[q] * hole[which][:, q * 128 : (q + 1) * 128] for q in range(2)], axis=1))
        return jnp.concatenate(parts, axis=0)

    def far(g, carry):
        tile_left(g).wait_recv()
        kb[0] += pick(lax.dot_general(h7[g], edge(recv_r, g, 0), NT, preferred_element_type=F32), 0)
        tile_right(g).wait_recv()
        kb[1] += pick(lax.dot_general(h0[g], edge(recv_l, g, 1), NT, preferred_element_type=F32), 0)
        return carry

    lax.fori_loop(0, NG, far, 0)

    mine = natural(folded(kb[0], kb[1]))
    c_s[...] = mine.astype(BF)

    def corner(n, where, to, slot):
        return pltpu.make_async_remote_copy(
            src_ref=c_s, dst_ref=c_r.at[slot], send_sem=s2.at[n], recv_sem=rs2.at[slot], device_id=(where, to), device_id_type=MESH
        )

    end = naux - 1
    corner(0, right, 0, naux + aux).start()
    corner(1, left, end, naux + aux).start()

    @pl.when(aux != 0)
    def _():
        corner(2, blk, 0, aux).start()

    @pl.when(aux != end)
    def _():
        corner(3, blk, end, aux).start()

    for cp in shares:
        cp.wait_recv()
    total = []
    for j in range(3):
        v = xf[2 * aux + j]
        for k in range(naux - 1):
            v = v + r1[k, j].astype(F32)
        total.append(v)

    def transposed(v):
        return jnp.concatenate([v, jnp.zeros((BS, 128), F32)], axis=0).T

    def store(n, j, v):
        out_ref[n * BS : (n + 1) * BS, j * BS : (j + 1) * BS] = v

    store(0, 0, transposed(total[0])[BS:128, 0:BS])
    store(0, 1, total[1][:, 0:BS])
    store(0, 2, total[1][:, BS:128])
    store(1, 0, transposed(total[1])[BS:128, 0:BS])
    store(1, 1, total[2][:, 0:BS])
    store(1, 2, total[2][:, BS:128])

    def boundary(own_half, slots):
        here, there = mine, jnp.zeros((BS, 128), F32)
        for slot in slots:
            corner(0, blk, 0, slot).wait_recv()
            here = here + c_r[slot].astype(F32)
        for slot in range(naux, 2 * naux):
            corner(0, blk, 0, slot).wait_recv()
            there = there + c_r[slot].astype(F32)
        other = transposed(there)
        if own_half == 1:
            return here[:, BS:128] + other[0:BS, 0:BS]
        return here[:, 0:BS] + other[BS:128, 0:BS]

    @pl.when(aux == 0)
    def _():
        store(0, 0, boundary(1, range(1, naux)))

    @pl.when(aux == end)
    def _():
        store(1, 2, boundary(0, range(end)))

    for h in halo:
        h.wait_send()
    for cp in shares:
        cp.wait_send()
    corner(0, right, 0, naux).wait_send()
    corner(1, left, end, naux).wait_send()

    @pl.when(aux != 0)
    def _():
        corner(2, blk, 0, aux).wait_send()

    @pl.when(aux != end)
    def _():
        corner(3, blk, end, aux).wait_send()

    def drain(g, carry):
        tile_left(g).wait_send()
        tile_right(g).wait_send()
        return carry

    lax.fori_loop(0, NG, drain, 0)


def solution(mesh):
    nblk, naux = mesh.shape["blk"], mesh.shape["aux"]

    def on_device(x, block_mask, density, density_mask):
        sem = pltpu.SemaphoreType.DMA
        return pl.pallas_call(
            functools.partial(kernel, nblk, naux),
            name="exchange",
            out_shape=jax.ShapeDtypeStruct((NB * BS // naux, 3 * BS), F32),
            in_specs=[
                pl.BlockSpec(memory_space=pl.ANY),
                pl.BlockSpec(memory_space=pltpu.SMEM),
                pl.BlockSpec(memory_space=pl.ANY),
                pl.BlockSpec(memory_space=pltpu.SMEM),
            ],
            out_specs=pl.BlockSpec(memory_space=pltpu.VMEM),
            scratch_shapes=[
                pltpu.VMEM(x.shape, BF),
                pltpu.VMEM(density.shape, BF),
                pltpu.VMEM((NB, CP, BS, 256), BF),
                pltpu.VMEM((NB, CP, BS, 256), BF),
                pltpu.VMEM((NG, CP * BS, 256), BF),
                pltpu.VMEM((NG, CP * BS, 256), BF),
                pltpu.VMEM((NG + 1, CP, 32, 384), BF),
                pltpu.VMEM((NG, CP, 32, 384), BF),
                pltpu.VMEM((NG, CP, 32, 384), BF),
                pltpu.VMEM((NG, CP, 32, 384), BF),
                pltpu.VMEM((NB + 1, 256, 256), BF),
                pltpu.VMEM((NB, 32, 256), BF),
                pltpu.VMEM((2, 32, 384), BF),
                pltpu.VMEM((2, BS, 128), BF),
                pltpu.VMEM((2, BS, 128), BF),
                pltpu.VMEM((NB, BS, 128), F32),
                pltpu.VMEM((NB, BS, 128), F32),
                pltpu.VMEM((2, BS, 128), F32),
                pltpu.VMEM((NB + 1, BS, 128), F32),
                pltpu.VMEM((NB + 1, BS, 128), BF),
                pltpu.VMEM((naux - 1, 3, BS, 128), BF),
                pltpu.VMEM((BS, 128), BF),
                pltpu.VMEM((2 * naux, BS, 128), BF),
                sem((NC,)), sem, sem((2,)), sem((2,)), sem((NG,)), sem((NG,)), sem((NG,)), sem((NG,)),
                sem((naux - 1,)), sem((naux - 1,)), sem((4,)), sem((2 * naux,)),
            ],
            compiler_params=pltpu.CompilerParams(
                collective_id=0, has_side_effects=True, vmem_limit_bytes=56 * 2**20
            ),
        )(x, block_mask, density, density_mask)

    placed = (P("aux", "blk", None), P("aux", "blk", None), P("blk", None), P("blk", None))
    return jax.shard_map(
        on_device, mesh=mesh, in_specs=placed, out_specs=P(("blk", "aux"), None), check_vma=False
    )
```

time: 333 us -> 66 us (0.20); the launches traced: 328 us -> 65.8 us
  local copies, waits for them, and re-layouts: 136 us -> 6.08 us
  waiting for transfers between devices: 73.6 us -> 0 us
  Pallas kernels: 0 us -> 59.7 us
  matrix products: 50.3 us -> 0 us
  other arithmetic: 37.8 us -> 0 us
  starting transfers between devices: 16.9 us -> 0 us
  between operations: 13.5 us -> 0.01 us
    pallas_call x0 -> x1, Pallas kernels: none -> 59.7 us  [on_device(): pl.pallas_call(functools.partial(kernel, nblk, naux), name='exchange', ou...]
    dot_general x16 -> x0, matrix products: 50.3 us -> none  [the longest x12 30.3 us: add_group(): jnp.einsum('qrms,qrns->rmn', piece, near_rows, preferred_element_type=jnp...]
    ppermute x4 -> x0, waiting for transfers between devices: 50 us -> none  [the longest x2 50 us: padded(): lax.ppermute(lax.slice_in_dim(block, block.shape[dim] - width, None, axis...]
    concatenate x1 -> x0, local copies, waits for them, and re-layouts: 47.5 us -> none  [padded(): block = jnp.concatenate([low, block, high], axis=dim)]
    reshape x2 -> x0, local copies, waits for them, and re-layouts: 38.1 us -> none  [the longest x1 37 us: on_device(): extended.reshape(aux_rows // sub_rows, sub_rows, extended.shape[1] * bloc...]
    mul x3 -> x0, other arithmetic: 24.2 us -> none  [the longest x1 23 us: on_device(): basis_three.reshape(groups, block_size, row_blocks, block_size, 3, block_...]
    unnamed x2 -> x0, waiting for transfers between devices: 23.6 us -> none
    slice x8 -> x0, local copies, waits for them, and re-layouts: 19.2 us -> none  [the longest x4 15.6 us: add_group(): aux_slab[:, first_row:first_row + row_count]]
  transfers between devices with their start and end apart: 5 -> 0, of which waited for: 2 -> 0; matrix products, arithmetic and copies ran while one was open for 4% -> 0% of each run, Pallas kernels for 0% -> 0%
where the time goes in v1:
time: 66 us; the launch traced here: 65.8 us
  Pallas kernels  59.7 us (90%)
  local copies, waits for them, and re-layouts  6.08 us (9%)
    pallas_call x1, Pallas kernels, on_device(): pl.pallas_call(functools.partial(kernel, nblk, naux), name='exchange', ou...  59.7 us
    unnamed x3, local copies, waits for them, and re-layouts  4.44 us
    pallas_call x1, local copies, waits for them, and re-layouts, on_device(): pl.pallas_call(functools.partial(kernel, nblk, naux), name='exchange', ou...  1.64 us

profile of v1, /device:TPU:0, one launch (start us, length us, event | category | flops | bytes accessed | tf_op | source)
XLA Modules:
  0.0 65.8 jit_solution(329415039348573383)
XLA Ops:
  0.0 1.3 %copy.5.bm_ref = s32[1,8,3]{2,1,0:T(8,128)} copy(s32[1,8,3]{1,0,2:T(1,128)} %param.5) | data formatting | bytes 192 | tf_op args[1]
  1.3 1.3 %copy.7.dm_ref = s32[8,3]{1,0:T(8,128)} copy(s32[8,3]{0,1:T(4,128)} %param.7) | data formatting | bytes 192 | tf_op args[3]
  2.7 1.8 %copy.6.d_hbm = bf16[512,192]{1,0:T(8,128)(2,1)} copy(bf16[512,192]{0,1:T(8,128)(2,1)} %param.6) | data formatting | bytes 393216 | tf_op args[2]
  4.4 59.7 %exchange.1 = f32[128,192]{1,0:T(8,128)} custom-call(bf16[64,8,12288]{2,1,0:T(8,128)(2,1)} %x_hbm.1, s32[1,8,3]{2,1,0:T(8,128)} %copy.5.bm_ref, bf16[512,192]{1,0:T(8,128)(2,1)} %copy.6.d_hbm, s32[8,3]{1,0:T(8,128)} %copy.7.dm_ref), custom_call_target="tpu_custom_call" | custom-call | tf_op jit(solution)/shard_map/exchange/pallas_call | solution.py:371
  64.2 1.6 %copy.8 = f32[128,192]{0,1:T(8,128)} copy(f32[128,192]{1,0:T(8,128)} %exchange.1) | data formatting | bytes 196608 | tf_op jit(solution)/shard_map/exchange/pallas_call | solution.py:371

commit v2 on v1

v2 whole, which is shorter than its diff:
```python
import functools

import jax
import jax.numpy as jnp
from jax import lax
from jax.experimental import pallas as pl
from jax.experimental.pallas import tpu as pltpu
from jax.sharding import PartitionSpec as P

MESH = pl.DeviceIdType.MESH
NT = (((1,), (1,)), ((), ()))
BF = jnp.bfloat16
F32 = jnp.float32

NB = 8
BS = 64
CP = 4
NC = 16
NG = NC // 2
ROW = 16


def first_place(b):
    return (b + 3) % 4


def aligned(cols, halves, place, low):
    turned = {}

    def at(half, side):
        col = half // 2
        if half % 2 == side:
            return cols[col]
        if col not in turned:
            turned[col] = pltpu.roll(cols[col], BS, 1)
        return turned[col]

    slots = [None] * 4
    for k, half in enumerate(halves):
        slots[(place + k) % 4] = half
    out = []
    for q in range(2):
        left, right = slots[2 * q], slots[2 * q + 1]
        if left is None:
            out.append(at(right, 1))
        elif right is None:
            out.append(at(left, 0))
        else:
            a, b = at(left, 0), at(right, 1)
            out.append(a if a is b else jnp.where(low, a, b))
    return out


def kernel(
    nblk, naux,
    x_hbm, bm_hbm, d_hbm, dm_hbm, out_ref,
    x_v, d_v, bm_ref, dm_ref, ta, tb, te, hx, send, recv, dens, mask, mask_s, halo_s, halo_r,
    k0, k1, kb, xf, xs, r1, mine, c_s, c_r,
    x_sem, d_sem, m_sem, hs, hr, bs, br, s1, rs1, s2, rs2,
):
    blk, aux = lax.axis_index("blk"), lax.axis_index("aux")
    right, left = lax.rem(blk + 1, nblk), lax.rem(blk + nblk - 1, nblk)

    def load(c):
        return pltpu.make_async_copy(x_hbm.at[pl.ds(c * CP, CP)], x_v.at[pl.ds(c * CP, CP)], x_sem.at[c])

    load(0).start()
    load(1).start()
    marks = (
        pltpu.make_async_copy(bm_hbm, bm_ref, m_sem.at[0]),
        pltpu.make_async_copy(dm_hbm, dm_ref, m_sem.at[1]),
    )
    for m in marks:
        m.start()

    barrier = pltpu.get_barrier_semaphore()
    for where in (left, blk, right):
        for k in range(naux):
            if where is blk and k == 0:
                continue
            pl.semaphore_signal(barrier, inc=1, device_id=(where, lax.rem(aux + k, naux)), device_id_type=MESH)

    density = pltpu.make_async_copy(d_hbm, d_v, d_sem)
    density.start()
    for c in range(2, NC):
        load(c).start()

    lane = lax.broadcasted_iota(jnp.int32, (32, 128), 1)
    low = lane < BS
    low64 = lax.broadcasted_iota(jnp.int32, (BS, 128), 1) < BS

    for m in marks:
        m.wait()

    def block_marks(b):
        return [bm_ref[j, 0, b].astype(F32) for j in range(3)]

    for s, b in enumerate((0, NB - 1)):
        m = block_marks(b)
        for q, (u, v) in enumerate(((0, 1), (2, 0), (1, 2))):
            mask_s[s, :, q * 128 : (q + 1) * 128] = jnp.where(low, m[u], m[v]).astype(BF)

    def to_left(src, dst, ss, rs):
        return pltpu.make_async_remote_copy(src_ref=src, dst_ref=dst, send_sem=ss, recv_sem=rs, device_id=(left, aux), device_id_type=MESH)

    def to_right(src, dst, ss, rs):
        return pltpu.make_async_remote_copy(src_ref=src, dst_ref=dst, send_sem=ss, recv_sem=rs, device_id=(right, aux), device_id_type=MESH)

    halo = (
        to_left(halo_s.at[0], halo_r.at[0], hs.at[0], hr.at[0]),
        to_right(halo_s.at[1], halo_r.at[1], hs.at[1], hr.at[1]),
    )

    def tile(side, g):
        return pltpu.make_async_remote_copy(
            src_ref=send.at[side, g], dst_ref=recv.at[1 - side, g], send_sem=bs.at[side, g], recv_sem=br.at[1 - side, g],
            device_id=(jnp.where(side == 0, left, right), aux), device_id_type=MESH,
        )

    def extract(g, which):
        for k in range(CP):
            rows = x_v[(2 * g + which) * CP + k].reshape(NB, 32, 384)
            send[which, g, k] = rows[(0, NB - 1)[which]] * mask_s[which]

    def spread(c, t):
        for k in range(CP):
            rows = x_v[c * CP + k].reshape(NB, 32, 384)
            for b in range(NB):
                u = rows[b]
                cols = [u[:, q * 128 : (q + 1) * 128] for q in range(3)]
                for par in range(2):
                    made = aligned(cols, [3 * par + n for n in range(3)], first_place(b), low)
                    for q in range(2):
                        rows_of, lanes = slice(par * 32, (par + 1) * 32), slice(q * 128, (q + 1) * 128)
                        v = made[q] * mask[b, :, lanes]
                        t[b, k, rows_of, lanes] = v
                        if b in (0, NB - 1):
                            te[b // (NB - 1), c, k, rows_of, lanes] = v

    def pick(o, base):
        s0 = jnp.where(low64, o[base : base + 64, 0:128], o[base + 64 : base + 128, 0:128])
        s1_ = jnp.where(low64, o[base + 128 : base + 192, 128:256], o[base + 192 : base + 256, 128:256])
        return s0 + s1_

    def product(left, tile):
        return lax.dot_general(left, tile, NT, preferred_element_type=F32)

    def halved(tile, slot):
        return jnp.dot(tile, dens[slot], preferred_element_type=F32).astype(BF)

    def multiply(t):
        before = None
        for b in range(NB):
            tile = t[b].reshape(CP * BS, 256)
            if b == NB - 1:
                k1[b - 1] += pick(product(before, tile), 0)
                continue
            half = halved(tile, b)
            if b > 0:
                o = product(jnp.concatenate([half, before], axis=0), tile)
                k0[b] += pick(o, 0)
                k1[b - 1] += pick(o, CP * BS)
            before = half

    def ends(g, carry):
        for c in range(2):
            first_tile = te[0, 2 * g + c].reshape(CP * BS, 256)
            last_tile = te[1, 2 * g + c].reshape(CP * BS, 256)
            first_half, last_half = halved(first_tile, NB), halved(last_tile, NB - 1)
            k0[0] += pick(product(first_half, first_tile), 0)
            k0[NB - 1] += pick(product(last_half, last_tile), 0)
            if c == 0:
                hx[1, g] = last_half
            else:
                hx[0, g] = first_half
        return carry

    for c in range(2):
        load(c).wait()
        extract(0, c)
        if c == 0:
            pl.semaphore_wait(barrier, 3 * naux - 1)
        tile(c, 0).start()

    density.wait()
    cols = []
    for j in range(3):
        cols.append([])
        for m in range(NB // 2):
            marks_of = jnp.where(low64, dm_ref[j, 2 * m].astype(F32), dm_ref[j, 2 * m + 1].astype(F32)).astype(BF)
            cols[j].append(d_v[j * BS : (j + 1) * BS, m * 128 : (m + 1) * 128] * marks_of)
    halo_s[0] = jnp.where(low64, cols[1][0], cols[0][0])
    halo_s[1] = jnp.where(low64, cols[2][-1], cols[1][-1])
    halo = (
        to_left(halo_s.at[0], halo_r.at[0], hs.at[0], hr.at[0]),
        to_right(halo_s.at[1], halo_r.at[1], hs.at[1], hr.at[1]),
    )

    for h in halo:
        h.start()

    def move(g, carry):
        for c in range(2):
            load(2 * g + c).wait()
            extract(g, c)
            tile(c, g).start()
        return carry

    lax.fori_loop(1, NG, move, 0)

    def lanes_of(values, place, rows):
        spot = lax.broadcasted_iota(jnp.int32, (rows, 256), 1) // BS
        total = jnp.zeros((rows, 256), F32)
        for j, value in enumerate(values):
            total = jnp.where(spot == (place + j) % 4, value, total)
        return total.astype(BF)

    for b in range(NB):
        mask[b] = lanes_of(block_marks(b), first_place(b), 32)
    hole = [lanes_of([1.0, 1.0, 1.0], first_place(b), 32) for b in (0, NB - 1)]

    k0[...] = jnp.zeros_like(k0)
    k1[...] = jnp.zeros_like(k1)
    kb[...] = jnp.zeros_like(kb)

    def turned(v):
        full = jnp.concatenate([v.astype(F32), jnp.zeros((BS, 128), F32)], axis=0).T
        return jnp.where(low64, full[0:BS], pltpu.roll(full[BS:128], BS, 1)).astype(BF)

    none = jnp.zeros((BS, 128), BF)
    after_t, ahead_t = turned(cols[2][-1]), turned(cols[0][0])
    after_t = pltpu.roll(after_t.astype(F32), BS, 1).astype(BF)
    ahead_t = pltpu.roll(ahead_t.astype(F32), BS, 1).astype(BF)

    def entry(l, c, after, ahead):
        j = l - c + 1
        if not 0 <= j <= 2:
            return none
        if 0 <= c < NB:
            return cols[j][c // 2]
        if c == NB:
            return (after_t, after)[l - NB + 1]
        if c == NB + 1:
            return after
        if c == -1:
            return (ahead, ahead_t)[l + 1]
        return ahead

    def second_factor(slot, b, columns, after, ahead):
        for l in range(b - 1, b + 3):
            for q in range(2):
                pair = [none if l == b + 2 else entry(l, c, after, ahead) for c in sorted(columns, key=lambda c: c % 4)[2 * q : 2 * q + 2]]
                made = none if pair[0] is none and pair[1] is none else jnp.where(low64, pair[0], pair[1])
                dens[slot, (l % 4) * BS : (l % 4 + 1) * BS, q * 128 : (q + 1) * 128] = made

    for b in range(NB - 1):
        second_factor(b, b, range(b - 1, b + 3), None, none)

    spread(0, ta)

    def step(g, carry):
        spread(2 * g + 1, tb)
        multiply(ta)
        spread(jnp.minimum(2 * g + 2, NC - 1), ta)
        multiply(tb)
        return carry

    lax.fori_loop(0, NG, step, 0)

    for h in halo:
        h.wait_recv()
    second_factor(NB - 1, NB - 1, range(NB - 2, NB + 2), halo_r[0], None)
    second_factor(NB, 0, range(-2, 2), None, halo_r[1])
    lax.fori_loop(0, NG, ends, 0)

    def folded(a, c):
        return jnp.where(low64, a + pltpu.roll(a, BS, 1), c + pltpu.roll(c, BS, 1))

    r = lax.broadcasted_iota(jnp.int32, (BS, 128), 0)
    c = lax.broadcasted_iota(jnp.int32, (BS, 128), 1)
    row_perm = jnp.where(r == 32 * (c % 2) + c // 2, 1.0, 0.0)[:, 0:BS]
    back = row_perm.T.astype(BF)
    r = lax.broadcasted_iota(jnp.int32, (128, 128), 0)
    c = lax.broadcasted_iota(jnp.int32, (128, 128), 1)
    lane_perm = jnp.where((r % BS == 32 * (c % 2) + (c % BS) // 2) & (r // BS == c // BS), 1.0, 0.0).astype(BF)

    def natural(v):
        v = jnp.dot(v.astype(BF), lane_perm, preferred_element_type=F32).astype(BF)
        return jnp.dot(back, v, preferred_element_type=F32)

    xs[0] = jnp.zeros((BS, 128), BF)
    xf[0] = jnp.zeros((BS, 128), F32)
    for b in range(NB):
        v = natural(folded(k0[b], k1[b]))
        xf[b + 1] = v
        xs[b + 1] = v.astype(BF)
    shares = []
    for k in range(1, naux):
        to = lax.rem(aux + k, naux)
        cp = pltpu.make_async_remote_copy(
            src_ref=xs.at[pl.ds(2 * to, 3)], dst_ref=r1.at[k - 1], send_sem=s1.at[k - 1], recv_sem=rs1.at[k - 1],
            device_id=(blk, to), device_id_type=MESH,
        )
        cp.start()
        shares.append(cp)

    def edge(side, g):
        parts = []
        for k in range(CP):
            u = recv[side, g, k]
            cols = [u[:, q * 128 : (q + 1) * 128] for q in range(3)]
            for par in range(2):
                made = aligned(cols, [3 * par + n for n in range(3)], first_place((NB - 1, 0)[side]), low)
                parts.append(jnp.concatenate([made[q] * hole[1 - side][:, q * 128 : (q + 1) * 128] for q in range(2)], axis=1))
        return jnp.concatenate(parts, axis=0)

    end = naux - 1

    def corner(n, where, to, slot):
        return pltpu.make_async_remote_copy(
            src_ref=c_s.at[n % 2], dst_ref=c_r.at[slot], send_sem=s2.at[n], recv_sem=rs2.at[slot], device_id=(where, to), device_id_type=MESH
        )

    def finish(sides):
        def far(g, carry):
            for side in sides:
                tile(1 - side, g).wait_recv()
                kb[side] += pick(product(hx[side, g], edge(side, g)), 0)
            return carry

        lax.fori_loop(0, NG, far, 0)
        v = natural(folded(kb[1], kb[0]))
        for side in sides:
            mine[side] = v
            c_s[side] = v.astype(BF)
        for side in sides:
            if side == 0:
                corner(0, left, end, naux + aux).start()
            else:
                corner(1, right, 0, naux + aux).start()

            @pl.when(aux != (0, end)[side])
            def _():
                corner(2 + side, blk, (0, end)[side], aux).start()

    last_of_row = lax.rem(blk, ROW) == ROW - 1

    @pl.when(last_of_row)
    def _():
        finish((1,))
        finish((0,))

    @pl.when(jnp.logical_not(last_of_row))
    def _():
        finish((0, 1))

    for cp in shares:
        cp.wait_recv()
    total = []
    for j in range(3):
        v = xf[2 * aux + j]
        for k in range(naux - 1):
            v = v + r1[k, j].astype(F32)
        total.append(v)

    out_ref[0:BS, :] = jnp.where(low64, pltpu.roll(total[0], BS, 1), total[1])
    out_ref[BS : 2 * BS, :] = jnp.where(low64, total[1], pltpu.roll(total[2], BS, 1))
    out_ref[2 * BS : 3 * BS, :] = jnp.concatenate(total[1:], axis=0).T[BS:128]

    def gathered(total, slots):
        for slot in slots:
            corner(0, blk, 0, slot).wait_recv()
            total = total + c_r[slot].astype(F32)
        return total

    def transposed(v):
        return jnp.concatenate([v, jnp.zeros((BS, 128), F32)], axis=0).T[:, 0:BS]

    nothing = jnp.zeros((BS, 128), F32)

    @pl.when(aux == 0)
    def _():
        own = transposed(gathered(mine[0], range(1, naux)))
        out_ref[0:BS, 0:BS] = own[BS:128] + gathered(nothing, range(naux, 2 * naux))[:, 0:BS]

    @pl.when(aux == end)
    def _():
        near = gathered(nothing, range(naux, 2 * naux))[:, BS:128]
        out_ref[2 * BS : 3 * BS, BS:128] = near + transposed(gathered(mine[1], range(end)))[0:BS]

    for h in halo:
        h.wait_send()
    for cp in shares:
        cp.wait_send()
    corner(0, left, end, naux).wait_send()
    corner(1, right, 0, naux).wait_send()

    @pl.when(aux != 0)
    def _():
        corner(2, blk, 0, aux).wait_send()

    @pl.when(aux != end)
    def _():
        corner(3, blk, end, aux).wait_send()

    def drain(g, carry):
        tile(0, g).wait_send()
        tile(1, g).wait_send()
        return carry

    lax.fori_loop(0, NG, drain, 0)


def solution(mesh):
    nblk, naux = mesh.shape["blk"], mesh.shape["aux"]

    def on_device(x, block_mask, density, density_mask):
        block_mask, density, density_mask = block_mask.transpose(2, 0, 1), density.T, density_mask.T
        sem = pltpu.SemaphoreType.DMA
        return pl.pallas_call(
            functools.partial(kernel, nblk, naux),
            name="exchange",
            out_shape=jax.ShapeDtypeStruct((3 * BS, NB * BS // naux), F32),
            in_specs=[pl.BlockSpec(memory_space=pl.ANY)] * 4,
            out_specs=pl.BlockSpec(memory_space=pltpu.VMEM),
            scratch_shapes=[
                pltpu.VMEM(x.shape, BF),
                pltpu.VMEM(density.shape, BF),
                pltpu.SMEM(block_mask.shape, jnp.int32),
                pltpu.SMEM(density_mask.shape, jnp.int32),
                pltpu.VMEM((NB, CP, BS, 256), BF),
                pltpu.VMEM((NB, CP, BS, 256), BF),
                pltpu.VMEM((2, NC, CP, BS, 256), BF),
                pltpu.VMEM((2, NG, CP * BS, 256), BF),
                pltpu.VMEM((2, NG, CP, 32, 384), BF),
                pltpu.VMEM((2, NG, CP, 32, 384), BF),
                pltpu.VMEM((NB + 1, 256, 256), BF),
                pltpu.VMEM((NB, 32, 256), BF),
                pltpu.VMEM((2, 32, 384), BF),
                pltpu.VMEM((2, BS, 128), BF),
                pltpu.VMEM((2, BS, 128), BF),
                pltpu.VMEM((NB, BS, 128), F32),
                pltpu.VMEM((NB, BS, 128), F32),
                pltpu.VMEM((2, BS, 128), F32),
                pltpu.VMEM((NB + 1, BS, 128), F32),
                pltpu.VMEM((NB + 1, BS, 128), BF),
                pltpu.VMEM((naux - 1, 3, BS, 128), BF),
                pltpu.VMEM((2, BS, 128), F32),
                pltpu.VMEM((2, BS, 128), BF),
                pltpu.VMEM((2 * naux, BS, 128), BF),
                sem((NC,)), sem, sem((2,)), sem((2,)), sem((2,)), sem((2, NG)), sem((2, NG)),
                sem((naux - 1,)), sem((naux - 1,)), sem((4,)), sem((2 * naux,)),
            ],
            compiler_params=pltpu.CompilerParams(
                collective_id=0, has_side_effects=True, vmem_limit_bytes=56 * 2**20
            ),
        )(x, block_mask, density, density_mask).T

    placed = (P("aux", "blk", None), P("aux", "blk", None), P("blk", None), P("blk", None))
    return jax.shard_map(
        on_device, mesh=mesh, in_specs=placed, out_specs=P(("blk", "aux"), None), check_vma=False
    )
```

time: 66 us -> 49 us (0.74)
  the two profiles are of different devices: /device:TPU:0 before, /device:TPU:232 now
where the time goes in v2:
time: 49 us; the launch traced here: 48.9 us
  Pallas kernels  47.4 us (97%)
  local copies, waits for them, and re-layouts  1.54 us (3%)
    pallas_call x1, Pallas kernels, on_device(): pl.pallas_call(functools.partial(kernel, nblk, naux), name='exchange', ou...  47.4 us
    unnamed x1, local copies, waits for them, and re-layouts  1.54 us

profile of v2, /device:TPU:232, one launch (start us, length us, event | category | flops | bytes accessed | tf_op | source)
XLA Modules:
  0.0 48.9 jit_solution(15363160687427248234)
XLA Ops:
  0.0 47.4 %exchange.1 = f32[192,128]{1,0:T(8,128)} custom-call(bf16[64,8,12288]{2,1,0:T(8,128)(2,1)} %x_hbm.1, s32[3,1,8]{2,1,0:T(1,128)} %bitcast.7, bf16[192,512]{1,0:T(8,128)(2,1)} %bitcast.5, s32[3,8]{1,0:T(4,128)} %bitcast.6), custom_call_target="tpu_custom_call" | custom-call | tf_op jit(solution)/shard_map/exchange/pallas_call | solution.py:420
  47.4 1.5 %copy.6 = f32[128,192]{0,1:T(8,128)} copy(f32[128,192]{0,1:T(8,128)} %bitcast.4) | data formatting | bytes 196608

commit v3 on v2

--- a/solution.py
+++ b/solution.py
@@ -56,7 +56,7 @@
     x_hbm, bm_hbm, d_hbm, dm_hbm, out_ref,
     x_v, d_v, bm_ref, dm_ref, ta, tb, te, hx, send, recv, dens, mask, mask_s, halo_s, halo_r,
     k0, k1, kb, xf, xs, r1, mine, c_s, c_r,
-    x_sem, d_sem, m_sem, hs, hr, bs, br, s1, rs1, s2, rs2,
+    x_sem, d_sem, m_sem, hs, hr, ps, pr, bs, br, s1, rs1, s2, rs2,
 ):
     blk, aux = lax.axis_index("blk"), lax.axis_index("aux")
     right, left = lax.rem(blk + 1, nblk), lax.rem(blk + nblk - 1, nblk)
@@ -105,11 +105,6 @@
 
     def to_right(src, dst, ss, rs):
         return pltpu.make_async_remote_copy(src_ref=src, dst_ref=dst, send_sem=ss, recv_sem=rs, device_id=(right, aux), device_id_type=MESH)
-
-    halo = (
-        to_left(halo_s.at[0], halo_r.at[0], hs.at[0], hr.at[0]),
-        to_right(halo_s.at[1], halo_r.at[1], hs.at[1], hr.at[1]),
-    )
 
     def tile(side, g):
         return pltpu.make_async_remote_copy(
@@ -191,10 +186,19 @@
             cols[j].append(d_v[j * BS : (j + 1) * BS, m * 128 : (m + 1) * 128] * marks_of)
     halo_s[0] = jnp.where(low64, cols[1][0], cols[0][0])
     halo_s[1] = jnp.where(low64, cols[2][-1], cols[1][-1])
+    core = lax.rem(aux, 2)
+    share = pl.ds(pl.multiple_of(core * 32, 32), 32)
     halo = (
-        to_left(halo_s.at[0], halo_r.at[0], hs.at[0], hr.at[0]),
-        to_right(halo_s.at[1], halo_r.at[1], hs.at[1], hr.at[1]),
+        to_left(halo_s.at[0, share], halo_r.at[0, share], hs.at[0], hr.at[0]),
+        to_right(halo_s.at[1, share], halo_r.at[1, share], hs.at[1], hr.at[1]),
     )
+    passed = [
+        pltpu.make_async_remote_copy(
+            src_ref=halo_r.at[n, share], dst_ref=halo_r.at[n, share], send_sem=ps.at[n], recv_sem=pr.at[n],
+            device_id=(blk, aux + 1 - 2 * core), device_id_type=MESH,
+        )
+        for n in range(2)
+    ]
 
     for h in halo:
         h.start()
@@ -267,8 +271,11 @@
 
     lax.fori_loop(0, NG, step, 0)
 
-    for h in halo:
+    for h, p in zip(halo, passed, strict=True):
         h.wait_recv()
+        p.start()
+    for p in passed:
+        p.wait()
     second_factor(NB - 1, NB - 1, range(NB - 2, NB + 2), halo_r[0], None)
     second_factor(NB, 0, range(-2, 2), None, halo_r[1])
     lax.fori_loop(0, NG, ends, 0)
@@ -350,7 +357,14 @@
         finish((1,))
         finish((0,))
 
-    @pl.when(jnp.logical_not(last_of_row))
+    middle_of_row = lax.rem(blk, ROW) == ROW // 2
+
+    @pl.when(middle_of_row)
+    def _():
+        finish((0,))
+        finish((1,))
+
+    @pl.when(jnp.logical_not(jnp.logical_or(last_of_row, middle_of_row)))
     def _():
         finish((0, 1))
 
@@ -420,7 +434,7 @@
         return pl.pallas_call(
             functools.partial(kernel, nblk, naux),
             name="exchange",
-            out_shape=jax.ShapeDtypeStruct((3 * BS, NB * BS // naux), F32),
+            out_shape=pltpu.VMEM((3 * BS, NB * BS // naux), F32),
             in_specs=[pl.BlockSpec(memory_space=pl.ANY)] * 4,
             out_specs=pl.BlockSpec(memory_space=pltpu.VMEM),
             scratch_shapes=[
@@ -448,7 +462,7 @@
                 pltpu.VMEM((2, BS, 128), F32),
                 pltpu.VMEM((2, BS, 128), BF),
                 pltpu.VMEM((2 * naux, BS, 128), BF),
-                sem((NC,)), sem, sem((2,)), sem((2,)), sem((2,)), sem((2, NG)), sem((2, NG)),
+                sem((NC,)), sem, sem((2,)), sem((2,)), sem((2,)), sem((2,)), sem((2,)), sem((2, NG)), sem((2, NG)),
                 sem((naux - 1,)), sem((naux - 1,)), sem((4,)), sem((2 * naux,)),
             ],
             compiler_params=pltpu.CompilerParams(

time: 49 us -> 47.2 us (0.963)
  the two profiles are of different devices: /device:TPU:232 before, /device:TPU:0 now
where the time goes in v3:
time: 47.2 us; the launch traced here: 46.5 us
  Pallas kernels  45.9 us (97%)
  local copies, waits for them, and re-layouts  0.64 us (1%)
    pallas_call x1, Pallas kernels, on_device(): pl.pallas_call(functools.partial(kernel, nblk, naux), name='exchange', ou...  45.9 us

profile of v3, /device:TPU:0, one launch (start us, length us, event | category | flops | bytes accessed | tf_op | source)
XLA Modules:
  0.0 46.5 jit_solution(759606702558183248)
XLA Ops:
  0.0 45.9 %exchange.1 = f32[192,128]{1,0:T(8,128)S(1)} custom-call(bf16[64,8,12288]{2,1,0:T(8,128)(2,1)} %x_hbm.1, s32[3,1,8]{2,1,0:T(1,128)} %bitcast.7, bf16[192,512]{1,0:T(8,128)(2,1)} %bitcast.5, s32[3,8]{1,0:T(4,128)} %bitcast.6), custom_call_target="tpu_custom_call" | custom-call | tf_op jit(solution)/shard_map/exchange/pallas_call | solution.py:434
  45.9 0.6 %copy.6 = f32[128,192]{0,1:T(8,128)} copy(f32[128,192]{0,1:T(8,128)S(1)} %bitcast.4) | data formatting | bytes 196608

commit v4 on v3

--- a/solution.py
+++ b/solution.py
@@ -17,7 +17,6 @@
 CP = 4
 NC = 16
 NG = NC // 2
-ROW = 16
 
 
 def first_place(b):
@@ -350,23 +349,17 @@
             def _():
                 corner(2 + side, blk, (0, end)[side], aux).start()
 
-    last_of_row = lax.rem(blk, ROW) == ROW - 1
-
-    @pl.when(last_of_row)
+    odd = lax.rem(blk, 2) == 1
+
+    @pl.when(odd)
     def _():
         finish((1,))
         finish((0,))
 
-    middle_of_row = lax.rem(blk, ROW) == ROW // 2
-
-    @pl.when(middle_of_row)
+    @pl.when(jnp.logical_not(odd))
     def _():
         finish((0,))
         finish((1,))
-
-    @pl.when(jnp.logical_not(jnp.logical_or(last_of_row, middle_of_row)))
-    def _():
-        finish((0, 1))
 
     for cp in shares:
         cp.wait_recv()
@@ -399,8 +392,8 @@
 
     @pl.when(aux == end)
     def _():
-        near = gathered(nothing, range(naux, 2 * naux))[:, BS:128]
-        out_ref[2 * BS : 3 * BS, BS:128] = near + transposed(gathered(mine[1], range(end)))[0:BS]
+        own = transposed(gathered(mine[1], range(end)))
+        out_ref[2 * BS : 3 * BS, BS:128] = own[0:BS] + gathered(nothing, range(naux, 2 * naux))[:, BS:128]
 
     for h in halo:
         h.wait_send()

time: 47.2 us -> 46.7 us (0.989); the launches traced: 46.5 us -> 46.5 us
  no operation moved by 1% of the time
where the time goes in v4:
time: 46.7 us; the launch traced here: 46.5 us
  Pallas kernels  45.9 us (98%)
  local copies, waits for them, and re-layouts  0.64 us (1%)
    pallas_call x1, Pallas kernels, on_device(): pl.pallas_call(functools.partial(kernel, nblk, naux), name='exchange', ou...  45.9 us

profile of v4, /device:TPU:0, one launch (start us, length us, event | category | flops | bytes accessed | tf_op | source)
XLA Modules:
  0.0 46.5 jit_solution(12364838272329882318)
XLA Ops:
  0.0 45.9 %exchange.1 = f32[192,128]{1,0:T(8,128)S(1)} custom-call(bf16[64,8,12288]{2,1,0:T(8,128)(2,1)} %x_hbm.1, s32[3,1,8]{2,1,0:T(1,128)} %bitcast.7, bf16[192,512]{1,0:T(8,128)(2,1)} %bitcast.5, s32[3,8]{1,0:T(4,128)} %bitcast.6), custom_call_target="tpu_custom_call" | custom-call | tf_op jit(solution)/shard_map/exchange/pallas_call | solution.py:427
  45.9 0.6 %copy.6 = f32[128,192]{0,1:T(8,128)} copy(f32[128,192]{0,1:T(8,128)S(1)} %bitcast.4) | data formatting | bytes 196608

commit v5 on v4

--- a/solution.py
+++ b/solution.py
@@ -156,6 +156,9 @@
                 k1[b - 1] += pick(o, CP * BS)
             before = half
 
+    def in_rows(half):
+        return jnp.dot(dens[NB + 1], half, preferred_element_type=F32).astype(BF)
+
     def ends(g, carry):
         for c in range(2):
             first_tile = te[0, 2 * g + c].reshape(CP * BS, 256)
@@ -164,9 +167,9 @@
             k0[0] += pick(product(first_half, first_tile), 0)
             k0[NB - 1] += pick(product(last_half, last_tile), 0)
             if c == 0:
-                hx[1, g] = last_half
+                hx[1, g] = in_rows(last_half)
             else:
-                hx[0, g] = first_half
+                hx[0, g] = in_rows(first_half)
         return carry
 
     for c in range(2):
@@ -277,6 +280,9 @@
         p.wait()
     second_factor(NB - 1, NB - 1, range(NB - 2, NB + 2), halo_r[0], None)
     second_factor(NB, 0, range(-2, 2), None, halo_r[1])
+    r = lax.broadcasted_iota(jnp.int32, (256, 256), 0)
+    c = lax.broadcasted_iota(jnp.int32, (256, 256), 1)
+    dens[NB + 1] = jnp.where((c % BS == 32 * (r % 2) + (r % BS) // 2) & (r // BS == c // BS), 1.0, 0.0).astype(BF)
     lax.fori_loop(0, NG, ends, 0)
 
     def folded(a, c):
@@ -335,7 +341,7 @@
             return carry
 
         lax.fori_loop(0, NG, far, 0)
-        v = natural(folded(kb[1], kb[0]))
+        v = jnp.dot(folded(kb[1], kb[0]).astype(BF), lane_perm, preferred_element_type=F32)
         for side in sides:
             mine[side] = v
             c_s[side] = v.astype(BF)
@@ -441,7 +447,7 @@
                 pltpu.VMEM((2, NG, CP * BS, 256), BF),
                 pltpu.VMEM((2, NG, CP, 32, 384), BF),
                 pltpu.VMEM((2, NG, CP, 32, 384), BF),
-                pltpu.VMEM((NB + 1, 256, 256), BF),
+                pltpu.VMEM((NB + 2, 256, 256), BF),
                 pltpu.VMEM((NB, 32, 256), BF),
                 pltpu.VMEM((2, 32, 384), BF),
                 pltpu.VMEM((2, BS, 128), BF),

time: 46.7 us -> 47.1 us (level)
  no operation moved by 1% of the time
where the time goes in v5:
time: 47.1 us; the launch traced here: 47 us
  Pallas kernels  46.3 us (98%)
  local copies, waits for them, and re-layouts  0.64 us (1%)
    pallas_call x1, Pallas kernels, on_device(): pl.pallas_call(functools.partial(kernel, nblk, naux), name='exchange', ou...  46.3 us

profile of v5, /device:TPU:0, one launch (start us, length us, event | category | flops | bytes accessed | tf_op | source)
XLA Modules:
  0.0 47.0 jit_solution(3873966354496406195)
XLA Ops:
  0.0 46.3 %exchange.1 = f32[192,128]{1,0:T(8,128)S(1)} custom-call(bf16[64,8,12288]{2,1,0:T(8,128)(2,1)} %x_hbm.1, s32[3,1,8]{2,1,0:T(1,128)} %bitcast.7, bf16[192,512]{1,0:T(8,128)(2,1)} %bitcast.5, s32[3,8]{1,0:T(4,128)} %bitcast.6), custom_call_target="tpu_custom_call" | custom-call | tf_op jit(solution)/shard_map/exchange/pallas_call | solution.py:433
  46.3 0.6 %copy.6 = f32[128,192]{0,1:T(8,128)} copy(f32[128,192]{0,1:T(8,128)S(1)} %bitcast.4) | data formatting | bytes 196608
